TPU v7x, 256 devices: a whole 4x4x8 slice. The times are simulated.
256 devices in a mesh: section: 4 (over y), node: 64 (over z, x, core).
Axes of the slice: x: 4, y: 4, z: 8, core: 2. Of those that a mesh axis runs over, the one named last changes fastest.
Arguments:
- master: float32 [4, 1024, 3072], P('section', 'node'), may hold values from -0.1875 to 0.1875
- first_moment: float32 [4, 1024, 3072], P('section', 'node'), may hold values from -6 to 6
- second_moment: float32 [4, 1024, 3072], P('section', 'node'), may hold values from 1 to 100
- node_state: bfloat16 [2, 4096, 1024], P(None, 'node'), may hold values from -6 to 6
- obs_rows: bfloat16 [2, 8192, 247], P(None, 'node'), may hold values from -6 to 6
- obs_device: int32 [2, 8192, 1], P(None, 'node'), may hold values from 0 to 63; in each aligned block of 128 rows (0 to 127, 128 to 255, ..., all dimensions but the last counted through in order) at most 4 rows name the same one
- obs_node: int32 [2, 8192], P(None, 'node'), may hold values from 0 to 63
- encode_weight: bfloat16 [247, 1024], replicated, may hold values from -0.375 to 0.375
- decode_weight: bfloat16 [1024, 247], replicated, may hold values from -0.1875 to 0.1875
- neighbors: int32 [4096, 16], P('node'), may hold values from 0 to 4095, as said below
- neighbor_count: int32 [4096], P('node'), may hold values from 1 to 16, as said below
- out_grad: bfloat16 [2, 4096, 247], P(None, 'node'), may hold values from -6 to 6
Outputs:
- new_weights: float32 [4, 1024, 3072], P('section', 'node')
- new_first: float32 [4, 1024, 3072], P('section', 'node')
- new_second: float32 [4, 1024, 3072], P('section', 'node')
Inputs may be any that keep to these rules, and one draw needn't show every extreme that they name: `obs_device`: in each micro-batch, the 128 profiles held by one index of node name one owner index at most 4 times. `neighbors`: the 16 ids of a node are distinct and each lies within 32 of the node's own id, counted cyclically over 4096 nodes. `neighbor_count`: slots at or past a node's count are padding.
All inputs are finite; a program needn't handle non-finite values.
Results may differ from a plain program's by a relative error of at most 0.015.
Values may be sent and summed in bfloat16 or wider, within the bound.
No kernel may reach another device: no remote copies, remote signals or barrier semaphores. Data moves between devices by JAX's collectives and lax.ppermute only.
A program may use at most 192 MiB of HBM per device.

v0:
```python
import jax
import jax.numpy as jnp
from jax import lax
from jax.experimental import pallas as pl
from jax.experimental.pallas import tpu as pltpu
from jax.sharding import Mesh, PartitionSpec as P

HEADS = 8
HALO_W = 32
STEP = 100


BETA_ONE = 0.9
BETA_TWO = 0.999
LEARN_RATE = 0.001

NODE = ("z", "x", "core")
PLANE = ("x", "core")
F32 = jnp.float32
BF16 = jnp.bfloat16
KERNEL_VMEM = 12 * 2**20


def across(index, count):
    return (index + 1) % count if index % 2 else (index - 1) % count


def swap(value):
    return lax.ppermute(value, "core", [(0, 1), (1, 0)])


def beside(value, steps):
    sections, count = lax.axis_size("section"), lax.axis_size(NODE)
    moves = [
        (section * count + index, (section + steps) * count + across(index, count))
        for section in range(sections)
        if 0 <= section + steps < sections
        for index in range(count)
    ]
    return lax.ppermute(value, ("section",) + NODE, moves)


def from_behind(value, axis, steps):
    count = lax.axis_size(axis)
    leading, last = (max(0, -steps), min(count, count - steps))
    return lax.ppermute(value, axis, [(source, source + steps) for source in range(leading, last)])


def norm_rows(values):
    return values * lax.rsqrt(jnp.mean(values * values, axis=-1, keepdims=True) + 1e-06)


def norm_pull(values, grads):
    scale = lax.rsqrt(jnp.mean(values * values, axis=-1, keepdims=True) + 1e-06)
    inner = jnp.mean(values * grads, axis=-1, keepdims=True)
    return scale * (grads - values * (inner * scale * scale))


def nt(a, b):
    return lax.dot_general(a, b, (((1,), (1,)), ((), ())), preferred_element_type=F32)


def nn(a, b):
    return lax.dot_general(a, b, (((1,), (0,)), ((), ())), preferred_element_type=F32)


def tn(a, b):
    return lax.dot_general(a, b, (((0,), (0,)), ((), ())), preferred_element_type=F32)


def spans(width, size):
    return [(start, start + size) for start in range(0, width, size)]


def rows_of(*pieces):
    return jnp.concatenate(pieces, axis=0)


def softmax_band(queries, keys, used, scale):
    scores = [nt(query, key) * scale for query, key in zip(queries, keys)]
    weights = [jnp.where(u, jnp.exp(score), 0.0) for u, score in zip(used, scores)]
    sums = [jnp.sum(weight, axis=-1, keepdims=True) for weight in weights]
    return [weight / total for weight, total in zip(weights, sums)]


def attend_kernel(side_ref, state_ref, proj_ref, mask_ref, out_ref):
    rows, width = state_ref.shape
    size = width // HEADS
    cuts = spans(width, size)
    half = rows // 2
    below = 2 - side_ref[0]
    above = 3 - below
    used = [mask_ref[...] > 0] * HEADS

    def banded(base):
        return [
            rows_of(
                proj_ref[below, half:, base + a : base + b],
                proj_ref[0, :, base + a : base + b],
                proj_ref[above, :half, base + a : base + b],
            )
            for a, b in cuts
        ]

    queries = [proj_ref[0, :, a:b] for a, b in cuts]
    probs = softmax_band(queries, banded(width), used, size ** (-0.5))
    mixed = [nn(p.astype(BF16), v) for p, v in zip(probs, banded(2 * width))]
    for (a, b), term in zip(cuts, mixed):
        out_ref[:, a:b] = (state_ref[:, a:b].astype(F32) + term).astype(BF16)


VMEM = pl.BlockSpec(memory_space=pltpu.VMEM)
SMEM = pl.BlockSpec(memory_space=pltpu.SMEM)


def attend(side, state, proj, mask):
    return pl.pallas_call(
        attend_kernel,
        out_shape=jax.ShapeDtypeStruct(state.shape, BF16),
        in_specs=[SMEM, VMEM, VMEM, VMEM],
        out_specs=VMEM,
        compiler_params=pltpu.CompilerParams(vmem_limit_bytes=KERNEL_VMEM),
        name="attend",
    )(side, state, proj, mask)


def pull_kernel(side_ref, proj_ref, mask_ref, own_ref, edge_ref, out_ref):
    rows, width = own_ref.shape
    size = width // HEADS
    scale = size ** (-0.5)
    cuts = spans(width, size)
    half = rows // 2
    below = 2 - side_ref[0]
    above = 3 - below

    def low_queries(a, b):
        return rows_of(proj_ref[below, half:, a:b], proj_ref[0, :half, a:b])

    def high_queries(a, b):
        return rows_of(proj_ref[0, half:, a:b], proj_ref[above, :half, a:b])

    def low_keys(a, b):
        return rows_of(proj_ref[below, :, a:b], proj_ref[0, :, a:b])

    def high_keys(a, b):
        return rows_of(proj_ref[0, :, a:b], proj_ref[above, :, a:b])

    def both(low, high, base):
        return [low(base + a, base + b) for a, b in cuts] + [
            high(base + a, base + b) for a, b in cuts
        ]

    queries = both(low_queries, high_queries, 0)
    keys = both(low_keys, high_keys, width)
    values = both(low_keys, high_keys, 2 * width)
    upstream = [rows_of(edge_ref[below - 1, :, a:b], own_ref[:half, a:b]) for a, b in cuts] + [
        rows_of(own_ref[half:, a:b], edge_ref[above - 1, :, a:b]) for a, b in cuts
    ]
    used = [mask_ref[0] > 0] * HEADS + [mask_ref[1] > 0] * HEADS
    probs = softmax_band(queries, keys, used, scale)
    grad_probs = [nt(u, v).astype(BF16).astype(F32) for u, v in zip(upstream, values)]
    inner = [jnp.sum(g * p, axis=-1, keepdims=True) for g, p in zip(grad_probs, probs)]
    grad_scores = [
        (p * (g - i) * scale).astype(BF16) for p, g, i in zip(probs, grad_probs, inner)
    ]
    rounded = [p.astype(BF16) for p in probs]
    for head, (a, b) in enumerate(cuts):
        low, high = head, HEADS + head
        out_ref[:half, a:b] = nn(grad_scores[low], keys[low])[half:].astype(BF16)
        out_ref[half:, a:b] = nn(grad_scores[high], keys[high])[:half].astype(BF16)
        for base, left, right in ((width, grad_scores, queries), (2 * width, rounded, upstream)):
            total = tn(left[low], right[low])[rows:] + tn(left[high], right[high])[:rows]
            out_ref[:, base + a : base + b] = total.astype(BF16)


def attend_pull(side, proj, masks, own, edges):
    return pl.pallas_call(
        pull_kernel,
        out_shape=jax.ShapeDtypeStruct(proj.shape[1:], BF16),
        in_specs=[SMEM, VMEM, VMEM, VMEM, VMEM],
        out_specs=VMEM,
        compiler_params=pltpu.CompilerParams(vmem_limit_bytes=KERNEL_VMEM),
        name="attend_pull",
    )(side, proj, masks, own, edges)


def route(obs_rows, obs_device, obs_node, encode_weight, node_state):
    micro, nodes_dev, width = node_state.shape
    per_dev, levels = obs_rows.shape[1:]
    node_devs = lax.axis_size(NODE)
    capacity = max(2, 2 * per_dev // node_devs)
    slots = node_devs * micro * capacity
    target = obs_device[..., 0]
    named = (target[..., None] == jnp.arange(node_devs)[None, None, :]).astype(BF16)
    earlier = (jnp.arange(per_dev)[:, None] > jnp.arange(per_dev)[None, :]).astype(BF16)
    before = jnp.einsum("ij,mjd->mid", earlier, named, preferred_element_type=F32)
    ranked = jnp.sum(before * named.astype(F32), axis=-1).astype(jnp.int32)
    position = (target * micro + jnp.arange(micro)[:, None]) * capacity + ranked
    chosen = (jnp.arange(slots)[:, None] == position.reshape(1, -1)).astype(BF16)
    payload = jnp.concatenate([obs_rows, obs_node[..., None].astype(BF16)], axis=-1)
    sent = nn(chosen, payload.reshape(micro * per_dev, levels + 1)).astype(BF16)
    received = lax.all_to_all(
        sent.reshape(node_devs, micro * capacity, levels + 1),
        NODE,
        split_axis=0,
        concat_axis=0,
        tiled=True,
    ).reshape(slots, levels + 1)
    owner = received[:, levels].astype(jnp.int32)
    owner = owner + (jnp.arange(slots) // capacity % micro) * nodes_dev
    held = (jnp.arange(micro * nodes_dev)[:, None] == owner[None, :]).astype(BF16)
    summed = nn(held, received[:, :levels])
    high = lax.reduce_precision(summed, 8, 7)
    rest = summed - high
    encoded = nn(high.astype(BF16), encode_weight) + nn(rest.astype(BF16), encode_weight)
    return (node_state.astype(F32) + encoded.reshape(micro, nodes_dev, width)).astype(BF16)


def body(
    master,
    first_moment,
    second_moment,
    node_state,
    obs_rows,
    obs_device,
    obs_node,
    encode_weight,
    decode_weight,
    neighbors,
    neighbor_count,
    out_grad,
):
    sections = lax.axis_size("section")
    section = lax.axis_index("section")
    node_devs = lax.axis_size(NODE)
    micro, nodes_dev, width = node_state.shape
    total_nodes = nodes_dev * node_devs
    anchor = lax.axis_index(NODE) * nodes_dev
    weight_full = lax.all_gather(master[0].astype(BF16), NODE, axis=0, tiled=True)
    core = lax.axis_index("core")
    side = core.astype(jnp.int32).reshape(1)
    half = nodes_dev // 2

    def pair_edge(value):
        return jnp.where(core == 0, value[..., half:, :], value[..., :half, :])

    def cross_edge(value):
        return jnp.where(core == 0, value[..., :half, :], value[..., half:, :])

    entry = route(obs_rows, obs_device, obs_node, encode_weight, node_state)
    rim = HALO_W
    relative = (neighbors - anchor) % total_nodes
    relative = jnp.where(relative >= total_nodes - rim, relative - total_nodes, relative) + rim
    relative = relative - half * (jnp.arange(nodes_dev)[:, None] // half)
    reach = half + 2 * rim
    valid = jnp.arange(neighbors.shape[1])[None, :] < neighbor_count[:, None]
    at = (relative[..., None] == jnp.arange(reach)[None, None, :]) & valid[..., None]
    near = jnp.sum(at.astype(F32), axis=1).astype(BF16)
    head_grad = nt(out_grad.reshape(micro * nodes_dev, -1), decode_weight)
    head_grad = head_grad.astype(BF16).reshape(micro, nodes_dev, width)

    def packed(edge):
        return jnp.concatenate(
            [edge(head_grad).reshape(-1, width), jnp.pad(edge(near), ((0, 0), (0, width - reach)))]
        )

    from_pair = swap(packed(pair_edge))
    from_cross = beside(jnp.concatenate([packed(cross_edge), entry.reshape(-1, width)]), 0)
    entry, from_pair, from_cross, head_grad = lax.optimization_barrier(
        (entry, from_pair, from_cross, head_grad)
    )
    heads = micro * half
    head_pair = from_pair[:heads].reshape(micro, half, width)
    head_cross = from_cross[:heads].reshape(micro, half, width)
    near_pair = from_pair[heads : heads + half, :reach]
    near_cross = from_cross[heads : heads + half, :reach]
    entry_cross = from_cross[heads + half :].reshape(micro, nodes_dev, width)
    near_low = jnp.where(core == 0, near_cross, near_pair)
    near_high = jnp.where(core == 0, near_pair, near_cross)

    def bands(upper, lower):
        room = 2 * nodes_dev - reach
        return jnp.concatenate(
            [jnp.pad(upper, ((0, 0), (0, room))), jnp.pad(lower, ((0, 0), (room, 0)))]
        ).astype(F32)

    mask = bands(near[:half], near[half:])
    masks = jnp.stack([bands(near_low, near[:half]), bands(near[half:], near_high)])

    ticks = micro + sections - 1
    incoming, incoming_cross = None, None
    saved = []
    kept_normed = [None] * micro
    for tick in range(ticks):
        state, cross = incoming, incoming_cross
        if tick == 0:
            state, cross = entry[0], entry_cross[0]
        elif tick < micro:
            state = jnp.where(section == 0, entry[tick], incoming)
            cross = jnp.where(section == 0, entry_cross[tick], incoming_cross)
        around = jnp.concatenate([state, swap(state), cross], axis=0)
        normed = norm_rows(around.astype(F32)).astype(BF16)
        proj = nn(normed, weight_full).astype(BF16).reshape(3, nodes_dev, 3 * width)
        saved.append((state, proj))
        for batch in range(micro):
            stage = tick - batch
            if stage == 0:
                kept_normed[batch] = normed[:nodes_dev]
            elif 0 < stage < sections:
                kept_normed[batch] = jnp.where(
                    section == stage, normed[:nodes_dev], kept_normed[batch]
                )
        if tick + 1 < ticks:
            output = attend(side, state, proj, mask)
            incoming_cross = beside(output, 1)
            incoming = from_behind(output, "section", 1)
    normed_all = lax.all_gather(jnp.stack(kept_normed), PLANE, axis=0, tiled=False)

    returning, returning_cross = None, None
    plane = lax.axis_size(PLANE)
    columns = 3 * width // plane
    kept_grad = [None] * micro
    for tick in range(ticks):
        sources = {}
        for stage in range(sections):
            batch = tick - (sections - 1) + stage
            if 0 <= batch < micro:
                sources[stage] = (batch, batch + stage)
        stages = sorted(sources)
        state, proj = saved[sources[stages[0]][1]]
        for stage in stages[1:]:
            here = section == stage
            state, proj = (
                jnp.where(here, a, b) for a, b in zip(saved[sources[stage][1]], (state, proj))
            )
        last = sections - 1
        if last not in sources:
            own, pair, cross = returning, swap(pair_edge(returning)), returning_cross
        elif tick == 0:
            own, pair, cross = head_grad[0], head_pair[0], head_cross[0]
        else:
            batch = sources[last][0]
            own = jnp.where(section == last, head_grad[batch], returning)
            cross = jnp.where(section == last, head_cross[batch], returning_cross)
            pair = swap(pair_edge(own))
        grad_qkv = attend_pull(side, proj, masks, own, jnp.stack([pair, cross]))
        for stage in stages:
            batch = sources[stage][0]
            if kept_grad[batch] is None:
                kept_grad[batch] = grad_qkv
            else:
                kept_grad[batch] = jnp.where(section == stage, grad_qkv, kept_grad[batch])
        if tick + 1 < ticks:
            grad_normed = nt(grad_qkv, weight_full)
            downward = (own.astype(F32) + norm_pull(state.astype(F32), grad_normed)).astype(BF16)
            returning_cross = beside(cross_edge(downward), -1)
            returning = from_behind(downward, "section", -1)
    parts = jnp.concatenate(kept_grad, axis=0).reshape(micro * nodes_dev, plane, columns)
    gathered = lax.all_to_all(
        parts.transpose(1, 0, 2), PLANE, split_axis=0, concat_axis=0, tiled=True
    )
    partial = tn(
        normed_all.reshape(plane * micro * nodes_dev, width),
        gathered.reshape(plane * micro * nodes_dev, columns),
    )
    rows = width // node_devs
    pieces = lax.all_to_all(
        partial.astype(BF16).reshape(node_devs, rows, columns),
        NODE,
        split_axis=0,
        concat_axis=0,
        tiled=True,
    )
    pieces = pieces.reshape(node_devs // plane, plane, rows, columns).astype(F32)
    gradient = jnp.sum(pieces, axis=0).transpose(1, 0, 2).reshape(1, rows, 3 * width)
    new_first = BETA_ONE * first_moment + (1.0 - BETA_ONE) * gradient
    new_second = BETA_TWO * second_moment + (1.0 - BETA_TWO) * gradient * gradient
    step_size = (
        new_first / (1.0 - BETA_ONE**STEP) / (jnp.sqrt(new_second / (1.0 - BETA_TWO**STEP)) + 1e-08)
    )
    new_weights = master - LEARN_RATE * step_size
    return (new_weights, new_first, new_second)


def solution(mesh):
    sections, node_devs = mesh.devices.shape
    fine = Mesh(mesh.devices.reshape(sections, node_devs // 8, 4, 2), ("section",) + NODE)
    in_specs = (
        P("section", NODE, None),
        P("section", NODE, None),
        P("section", NODE, None),
        P(None, NODE, None),
        P(None, NODE, None),
        P(None, NODE, None),
        P(None, NODE),
        P(),
        P(),
        P(NODE, None),
        P(NODE),
        P(None, NODE, None),
    )
    out_specs = (P("section", NODE, None), P("section", NODE, None), P("section", NODE, None))
    return jax.shard_map(body, mesh=fine, in_specs=in_specs, out_specs=out_specs, check_vma=False)
```

profile of v0, /device:TPU:8, one launch (start us, length us, event | category | flops | bytes accessed | tf_op | source)
XLA Modules:
  0.0 295.0 jit_solution(3337453706489623173)
XLA Ops:
  13.4 11.9 %all-to-all-start = ((bf16[64,8,248]{2,1,0:T(8,128)(2,1)}), bf16[64,8,248]{2,1,0:T(8,128)(2,1)S(1)}, u32[]{:S(2)}, u32[]{:S(2)}) async-start(bf16[64,8,248]{2,1,0:T(8,128)(2,1)} %bitcast.7), calls=%async_computation | async-start | bytes 524288 | tf_op jit(solution)/shard_map/all_to_all | solution.py:202
  27.1 11.9 %all-to-all-done = bf16[64,8,248]{2,1,0:T(8,128)(2,1)S(1)} async-done(((bf16[64,8,248]{2,1,0:T(8,128)(2,1)}), bf16[64,8,248]{2,1,0:T(8,128)(2,1)S(1)}, u32[]{:S(2)}, u32[]{:S(2)}) %all-to-all-start) | async-done | bytes 253984 | tf_op jit(solution)/shard_map/all_to_all | solution.py:202
  43.2 9.2 %collective-permute-done.1 = bf16[224,1024]{1,0:T(8,128)(2,1)S(1)} collective-permute-done((bf16[224,1024]{1,0:T(8,128)(2,1)S(1)}, bf16[224,1024]{1,0:T(8,128)(2,1)S(1)}, u32[]{:S(2)}, u32[]{:S(2)}) %collective-permute-start.1) | collective-permute-done | bytes 458784 | tf_op jit(solution)/shard_map/ppermute | solution.py:40
  54.2 41.3 %all-gather.5.cloned.1.call-done = bf16[1,1024,3072]{2,1,0:T(8,128)(2,1)} async-done(((bf16[1,16,3072]{2,1,0:T(8,128)(2,1)}), bf16[1,1024,3072]{2,1,0:T(8,128)(2,1)}) %all-gather.5.cloned.1.call-update) | async-done | bytes 6291472 | tf_op jit(solution)/shard_map/all_gather | solution.py:239
  95.6 4.2 %fusion.18 = bf16[192,3072]{1,0:T(8,128)(2,1)S(1)} fusion(bf16[192,1024]{1,0:T(8,128)(2,1)S(1)} %fusion.38, bf16[1,1024,3072]{2,1,0:T(8,128)(2,1)} %all-gather.5.cloned.1.call-done), kind=kOutput, calls=%fused_computation.18 | convolution fusion | flops 1208549376 | bytes 7864320 | tf_op jit(solution)/shard_map/dot_general | solution.py:64
  100.3 3.4 %collective-permute-start.3 = (bf16[64,1024]{1,0:T(8,128)(2,1)S(1)}, bf16[64,1024]{1,0:T(8,128)(2,1)S(1)}, u32[]{:S(2)}, u32[]{:S(2)}) collective-permute-start(bf16[64,1024]{1,0:T(8,128)(2,1)S(1)} %attend.4), channel_id=1, source_target_pairs={{0,64},{64,128},{128,192},{1,65},{65,129},{129,193},{2,66},{66,130... | collective-permute-start | bytes 393224 | tf_op jit(solution)/shard_map/ppermute | solution.py:46
  103.8 4.4 %collective-permute-start.5 = (bf16[64,1024]{1,0:T(8,128)(2,1)S(1)}, bf16[64,1024]{1,0:T(8,128)(2,1)S(1)}, u32[]{:S(2)}, u32[]{:S(2)}) collective-permute-start(bf16[64,1024]{1,0:T(8,128)(2,1)S(1)} %attend.4), channel_id=1, source_target_pairs={{0,127},{1,66},{2,65},{3,68},{4,67},{5,70},{6,69},{7,72},{8,71},{9... | collective-permute-start | bytes 393224 | tf_op jit(solution)/shard_map/ppermute | solution.py:40
  108.4 5.9 %collective-permute-done.5 = bf16[64,1024]{1,0:T(8,128)(2,1)S(1)} collective-permute-done((bf16[64,1024]{1,0:T(8,128)(2,1)S(1)}, bf16[64,1024]{1,0:T(8,128)(2,1)S(1)}, u32[]{:S(2)}, u32[]{:S(2)}) %collective-permute-start.5) | collective-permute-done | bytes 131104 | tf_op jit(solution)/shard_map/ppermute | solution.py:40
  114.7 4.4 %fusion.21 = bf16[192,3072]{1,0:T(8,128)(2,1)S(1)} fusion(bf16[192,1024]{1,0:T(8,128)(2,1)S(1)} %fusion.40, bf16[1,1024,3072]{2,1,0:T(8,128)(2,1)} %all-gather.5.cloned.1.call-done), kind=kOutput, calls=%fused_computation.19 | convolution fusion | flops 1208549376 | bytes 7864320 | tf_op jit(solution)/shard_map/dot_general | solution.py:64
  123.6 3.2 %collective-permute-start.8 = (bf16[64,1024]{1,0:T(8,128)(2,1)S(1)}, bf16[64,1024]{1,0:T(8,128)(2,1)S(1)}, u32[]{:S(2)}, u32[]{:S(2)}) collective-permute-start(bf16[64,1024]{1,0:T(8,128)(2,1)S(1)} %attend.5), channel_id=1, source_target_pairs={{0,127},{1,66},{2,65},{3,68},{4,67},{5,70},{6,69},{7,72},{8,71},{9... | collective-permute-start | bytes 393224 | tf_op jit(solution)/shard_map/ppermute | solution.py:40
  127.9 6.2 %collective-permute-done.8 = bf16[64,1024]{1,0:T(8,128)(2,1)S(1)} collective-permute-done((bf16[64,1024]{1,0:T(8,128)(2,1)S(1)}, bf16[64,1024]{1,0:T(8,128)(2,1)S(1)}, u32[]{:S(2)}, u32[]{:S(2)}) %collective-permute-start.8) | collective-permute-done | bytes 131104 | tf_op jit(solution)/shard_map/ppermute | solution.py:40
  144.1 5.5 %collective-permute-done.11 = bf16[64,1024]{1,0:T(8,128)(2,1)S(1)} collective-permute-done((bf16[64,1024]{1,0:T(8,128)(2,1)S(1)}, bf16[64,1024]{1,0:T(8,128)(2,1)S(1)}, u32[]{:S(2)}, u32[]{:S(2)}) %collective-permute-start.11) | collective-permute-done | bytes 131104 | tf_op jit(solution)/shard_map/ppermute | solution.py:40
  157.7 3.9 %collective-permute-start.12 = (bf16[64,1024]{1,0:T(8,128)(2,1)S(1)}, bf16[64,1024]{1,0:T(8,128)(2,1)S(1)}, u32[]{:S(2)}, u32[]{:S(2)}) collective-permute-start(bf16[64,1024]{1,0:T(8,128)(2,1)S(1)} %attend.7), channel_id=1, source_target_pairs={{0,64},{64,128},{128,192},{1,65},{65,129},{129,193},{2,66},{66,130... | collective-permute-start | bytes 393224 | tf_op jit(solution)/shard_map/ppermute | solution.py:46
  164.3 7.1 %collective-permute-start.17 = (bf16[32,1024]{1,0:T(8,128)(2,1)S(1)}, bf16[32,1024]{1,0:T(8,128)(2,1)S(1)}, u32[]{:S(2)}, u32[]{:S(2)}) collective-permute-start(bf16[32,1024]{1,0:T(8,128)(2,1)S(1)} %slice_select_fusion.9), channel_id=1, source_target_pairs={{64,63},{65,2},{66,1},{67,4},{68,3},{69,6},{70,5},{71,8},{72,7},{7... | collective-permute-start | bytes 196616 | tf_op jit(solution)/shard_map/ppermute | solution.py:40
  182.5 3.8 %collective-permute-start.18 = (bf16[64,1024]{1,0:T(8,128)(2,1)S(1)}, bf16[64,1024]{1,0:T(8,128)(2,1)S(1)}, u32[]{:S(2)}, u32[]{:S(2)}) collective-permute-start(bf16[64,1024]{1,0:T(8,128)(2,1)S(1)} %fusion.62), channel_id=1, source_target_pairs={{64,0},{128,64},{192,128},{65,1},{129,65},{193,129},{66,2},{130,66... | collective-permute-start | bytes 393224 | tf_op jit(solution)/shard_map/ppermute | solution.py:46
  187.0 4.7 %collective-permute-start.20 = (bf16[32,1024]{1,0:T(8,128)(2,1)}, bf16[32,1024]{1,0:T(8,128)(2,1)}, u32[]{:S(2)}, u32[]{:S(2)}) collective-permute-start(bf16[32,1024]{1,0:T(8,128)(2,1)} %slice_select_fusion.7), channel_id=1, source_target_pairs={{64,63},{65,2},{66,1},{67,4},{68,3},{69,6},{70,5},{71,8},{72,7},{7... | collective-permute-start | bytes 196616 | tf_op jit(solution)/shard_map/ppermute | solution.py:40
  201.3 5.2 %fusion.63 = (f32[64]{0:T(128)S(1)}, f32[64]{0:T(128)S(1)}, bf16[64,1024]{1,0:T(8,128)(2,1)S(1)}, f32[64,1024]{1,0:T(8,128)S(1)}) fusion(bf16[64,1024]{1,0:T(8,128)(2,1)S(1)} %collective-permute-done.9.state_ref, bf16[64,1024]{1,0:T(8,128)(2,1)} %copy-done.5, pred[]{:T(512)S(6)} %eq.56, bf16[64,3072]{1,0:T(8,128)(2,1)S(1)} %attend_pull.7, ...), kind=kOutput, calls=%fused_computation.101 | convolution fusion | flops 403046272 | bytes 7340545 | tf_op jit(solution)/shard_map/dot_general | solution.py:60
  208.6 4.0 %collective-permute-start.23 = (bf16[32,1024]{1,0:T(8,128)(2,1)S(1)}, bf16[32,1024]{1,0:T(8,128)(2,1)S(1)}, u32[]{:S(2)}, u32[]{:S(2)}) collective-permute-start(bf16[32,1024]{1,0:T(8,128)(2,1)S(1)} %slice_select_fusion.5), channel_id=1, source_target_pairs={{64,63},{65,2},{66,1},{67,4},{68,3},{69,6},{70,5},{71,8},{72,7},{7... | collective-permute-start | bytes 196616 | tf_op jit(solution)/shard_map/ppermute | solution.py:40
  213.9 4.6 %collective-permute-done.23 = bf16[32,1024]{1,0:T(8,128)(2,1)S(1)} collective-permute-done((bf16[32,1024]{1,0:T(8,128)(2,1)S(1)}, bf16[32,1024]{1,0:T(8,128)(2,1)S(1)}, u32[]{:S(2)}, u32[]{:S(2)}) %collective-permute-start.23) | collective-permute-done | bytes 65568 | tf_op jit(solution)/shard_map/ppermute | solution.py:40
  220.0 4.9 %fusion.69 = (f32[64]{0:T(128)S(1)}, f32[64]{0:T(128)S(1)}, bf16[64,1024]{1,0:T(8,128)(2,1)S(1)}, f32[64,1024]{1,0:T(8,128)S(1)}) fusion(bf16[64,1024]{1,0:T(8,128)(2,1)S(1)} %collective-permute-done.6.state_ref, bf16[2,64,1024]{2,1,0:T(8,128)(2,1)S(1)} %copy-done.13, pred[]{:T(512)S(6)} %eq.57, bf16[64,3072]{1,0:T(8,128)(2,1)S(1)} %attend_pull.8, ...), kind=kOutput, calls=%fused_computation.107 | convolution fusion | flops 403046272 | bytes 7340545 | tf_op jit(solution)/shard_map/dot_general | solution.py:60
  227.1 3.4 %collective-permute-start.26 = (bf16[32,1024]{1,0:T(8,128)(2,1)S(1)}, bf16[32,1024]{1,0:T(8,128)(2,1)S(1)}, u32[]{:S(2)}, u32[]{:S(2)}) collective-permute-start(bf16[32,1024]{1,0:T(8,128)(2,1)S(1)} %slice_select_fusion.3), channel_id=1, source_target_pairs={{64,63},{65,2},{66,1},{67,4},{68,3},{69,6},{70,5},{71,8},{72,7},{7... | collective-permute-start | bytes 196616 | tf_op jit(solution)/shard_map/ppermute | solution.py:40
  232.1 4.7 %collective-permute-done.26 = bf16[32,1024]{1,0:T(8,128)(2,1)S(1)} collective-permute-done((bf16[32,1024]{1,0:T(8,128)(2,1)S(1)}, bf16[32,1024]{1,0:T(8,128)(2,1)S(1)}, u32[]{:S(2)}, u32[]{:S(2)}) %collective-permute-start.26) | collective-permute-done | bytes 65568 | tf_op jit(solution)/shard_map/ppermute | solution.py:40
  238.7 15.7 %all_to_all.15 = bf16[8,128,384]{2,1,0:T(8,128)(2,1)S(1)} all-to-all(bf16[8,128,384]{2,1,0:T(8,128)(2,1)S(1)} %bitcast.166), channel_id=1, replica_groups=mesh['section'=4,'z'=8,'x'=4,'core'=2] {'x','core'}, dimensions={0} | all-to-all | bytes 1572864 | tf_op jit(solution)/shard_map/all_to_all | solution.py:359
  257.3 29.7 %all_to_all.16 = bf16[64,16,384]{2,1,0:T(8,128)(2,1)S(1)} all-to-all(bf16[64,16,384]{2,1,0:T(8,128)(2,1)S(1)} %bitcast.171), channel_id=1, replica_groups=mesh['section'=4,'z'=8,'x'=4,'core'=2] {'z','x','core'}, dimensions={0} | all-to-all | bytes 1572864 | tf_op jit(solution)/shard_map/all_to_all | solution.py:367
  (212 shorter events, 76.5 us)
Async XLA Ops:
  7.2 88.3 %all-gather.5.cloned.1.call-start = ((), (), s32[]{:S(2)}) async-start(), calls=%async_computation.3 | async-start | bytes 6389760 | tf_op jit(solution)/shard_map/all_gather | solution.py:239
  13.4 25.5 %all-to-all-start = ((bf16[64,8,248]{2,1,0:T(8,128)(2,1)}), bf16[64,8,248]{2,1,0:T(8,128)(2,1)S(1)}, u32[]{:S(2)}, u32[]{:S(2)}) async-start(bf16[64,8,248]{2,1,0:T(8,128)(2,1)} %bitcast.7), calls=%async_computation | async-start | bytes 524288 | tf_op jit(solution)/shard_map/all_to_all | solution.py:202
  25.4 229.0 %all-gather.7.cloned.1.call-start = ((), (), s32[]{:S(2)}) async-start(), calls=%async_computation.4 | async-start | bytes 2359296 | tf_op jit(solution)/shard_map/all_gather | solution.py:317
  40.1 12.3 %collective-permute-start.1 = (bf16[224,1024]{1,0:T(8,128)(2,1)S(1)}, bf16[224,1024]{1,0:T(8,128)(2,1)S(1)}, u32[]{:S(2)}, u32[]{:S(2)}) collective-permute-start(bf16[224,1024]{1,0:T(8,128)(2,1)S(1)} %fusion.49), channel_id=1, source_target_pairs={{0,63},{1,2},{2,1},{3,4},{4,3},{5,6},{6,5},{7,8},{8,7},{9,10},{10,... | collective-permute-start | bytes 1376264 | tf_op jit(solution)/shard_map/ppermute | solution.py:40
  100.3 7.9 %collective-permute-start.3 = (bf16[64,1024]{1,0:T(8,128)(2,1)S(1)}, bf16[64,1024]{1,0:T(8,128)(2,1)S(1)}, u32[]{:S(2)}, u32[]{:S(2)}) collective-permute-start(bf16[64,1024]{1,0:T(8,128)(2,1)S(1)} %attend.4), channel_id=1, source_target_pairs={{0,64},{64,128},{128,192},{1,65},{65,129},{129,193},{2,66},{66,130... | collective-permute-start | bytes 393224 | tf_op jit(solution)/shard_map/ppermute | solution.py:46
  103.8 10.5 %collective-permute-start.5 = (bf16[64,1024]{1,0:T(8,128)(2,1)S(1)}, bf16[64,1024]{1,0:T(8,128)(2,1)S(1)}, u32[]{:S(2)}, u32[]{:S(2)}) collective-permute-start(bf16[64,1024]{1,0:T(8,128)(2,1)S(1)} %attend.4), channel_id=1, source_target_pairs={{0,127},{1,66},{2,65},{3,68},{4,67},{5,70},{6,69},{7,72},{8,71},{9... | collective-permute-start | bytes 393224 | tf_op jit(solution)/shard_map/ppermute | solution.py:40
  108.3 6.1 %collective-permute-start.4 = (bf16[64,1024]{1,0:T(8,128)(2,1)S(1)}, bf16[64,1024]{1,0:T(8,128)(2,1)S(1)}, u32[]{:S(2)}, u32[]{:S(2)}) collective-permute-start(bf16[64,1024]{1,0:T(8,128)(2,1)S(1)} %bitcast_select_fusion.1.state_ref), channel_id=1, source_target_pairs={{0,1},{1,0},{2,3},{3,2},{4,5},{5,4},{6,7},{7,6},{8,9},{9,8},{10,11... | collective-permute-start | bytes 393224 | tf_op jit(solution)/shard_map/ppermute | solution.py:29
  119.6 8.3 %collective-permute-start.6 = (bf16[64,1024]{1,0:T(8,128)(2,1)S(1)}, bf16[64,1024]{1,0:T(8,128)(2,1)S(1)}, u32[]{:S(2)}, u32[]{:S(2)}) collective-permute-start(bf16[64,1024]{1,0:T(8,128)(2,1)S(1)} %attend.5), channel_id=1, source_target_pairs={{0,64},{64,128},{128,192},{1,65},{65,129},{129,193},{2,66},{66,130... | collective-permute-start | bytes 393224 | tf_op jit(solution)/shard_map/ppermute | solution.py:46
  123.6 10.5 %collective-permute-start.8 = (bf16[64,1024]{1,0:T(8,128)(2,1)S(1)}, bf16[64,1024]{1,0:T(8,128)(2,1)S(1)}, u32[]{:S(2)}, u32[]{:S(2)}) collective-permute-start(bf16[64,1024]{1,0:T(8,128)(2,1)S(1)} %attend.5), channel_id=1, source_target_pairs={{0,127},{1,66},{2,65},{3,68},{4,67},{5,70},{6,69},{7,72},{8,71},{9... | collective-permute-start | bytes 393224 | tf_op jit(solution)/shard_map/ppermute | solution.py:40
  127.8 6.2 %collective-permute-start.7 = (bf16[64,1024]{1,0:T(8,128)(2,1)S(1)}, bf16[64,1024]{1,0:T(8,128)(2,1)S(1)}, u32[]{:S(2)}, u32[]{:S(2)}) collective-permute-start(bf16[64,1024]{1,0:T(8,128)(2,1)S(1)} %collective-permute-done.6.state_ref), channel_id=1, source_target_pairs={{0,1},{1,0},{2,3},{3,2},{4,5},{5,4},{6,7},{7,6},{8,9},{9,8},{10,11... | collective-permute-start | bytes 393224 | tf_op jit(solution)/shard_map/ppermute | solution.py:29
  136.4 7.7 %collective-permute-start.9 = (bf16[64,1024]{1,0:T(8,128)(2,1)S(1)}, bf16[64,1024]{1,0:T(8,128)(2,1)S(1)}, u32[]{:S(2)}, u32[]{:S(2)}) collective-permute-start(bf16[64,1024]{1,0:T(8,128)(2,1)S(1)} %attend.6), channel_id=1, source_target_pairs={{0,64},{64,128},{128,192},{1,65},{65,129},{129,193},{2,66},{66,130... | collective-permute-start | bytes 393224 | tf_op jit(solution)/shard_map/ppermute | solution.py:46
  139.1 10.5 %collective-permute-start.11 = (bf16[64,1024]{1,0:T(8,128)(2,1)S(1)}, bf16[64,1024]{1,0:T(8,128)(2,1)S(1)}, u32[]{:S(2)}, u32[]{:S(2)}) collective-permute-start(bf16[64,1024]{1,0:T(8,128)(2,1)S(1)} %attend.6), channel_id=1, source_target_pairs={{0,127},{1,66},{2,65},{3,68},{4,67},{5,70},{6,69},{7,72},{8,71},{9... | collective-permute-start | bytes 393224 | tf_op jit(solution)/shard_map/ppermute | solution.py:40
  144.0 5.6 %collective-permute-start.10 = (bf16[64,1024]{1,0:T(8,128)(2,1)S(1)}, bf16[64,1024]{1,0:T(8,128)(2,1)S(1)}, u32[]{:S(2)}, u32[]{:S(2)}) collective-permute-start(bf16[64,1024]{1,0:T(8,128)(2,1)S(1)} %collective-permute-done.9.state_ref), channel_id=1, source_target_pairs={{0,1},{1,0},{2,3},{3,2},{4,5},{5,4},{6,7},{7,6},{8,9},{9,8},{10,11... | collective-permute-start | bytes 393224 | tf_op jit(solution)/shard_map/ppermute | solution.py:29
  155.2 17.4 %collective-permute-start.15 = (bf16[64,1024]{1,0:T(8,128)(2,1)S(1)}, bf16[64,1024]{1,0:T(8,128)(2,1)S(1)}, u32[]{:S(2)}, u32[]{:S(2)}) collective-permute-start(bf16[64,1024]{1,0:T(8,128)(2,1)S(1)} %fusion.56), channel_id=1, source_target_pairs={{64,0},{128,64},{192,128},{65,1},{129,65},{193,129},{66,2},{130,66... | collective-permute-start | bytes 393224 | tf_op jit(solution)/shard_map/ppermute | solution.py:46
  157.7 15.1 %collective-permute-start.12 = (bf16[64,1024]{1,0:T(8,128)(2,1)S(1)}, bf16[64,1024]{1,0:T(8,128)(2,1)S(1)}, u32[]{:S(2)}, u32[]{:S(2)}) collective-permute-start(bf16[64,1024]{1,0:T(8,128)(2,1)S(1)} %attend.7), channel_id=1, source_target_pairs={{0,64},{64,128},{128,192},{1,65},{65,129},{129,193},{2,66},{66,130... | collective-permute-start | bytes 393224 | tf_op jit(solution)/shard_map/ppermute | solution.py:46
  161.6 13.4 %collective-permute-start.14 = (bf16[64,1024]{1,0:T(8,128)(2,1)S(1)}, bf16[64,1024]{1,0:T(8,128)(2,1)S(1)}, u32[]{:S(2)}, u32[]{:S(2)}) collective-permute-start(bf16[64,1024]{1,0:T(8,128)(2,1)S(1)} %attend.7), channel_id=1, source_target_pairs={{0,127},{1,66},{2,65},{3,68},{4,67},{5,70},{6,69},{7,72},{8,71},{9... | collective-permute-start | bytes 393224 | tf_op jit(solution)/shard_map/ppermute | solution.py:40
  164.3 9.8 %collective-permute-start.17 = (bf16[32,1024]{1,0:T(8,128)(2,1)S(1)}, bf16[32,1024]{1,0:T(8,128)(2,1)S(1)}, u32[]{:S(2)}, u32[]{:S(2)}) collective-permute-start(bf16[32,1024]{1,0:T(8,128)(2,1)S(1)} %slice_select_fusion.9), channel_id=1, source_target_pairs={{64,63},{65,2},{66,1},{67,4},{68,3},{69,6},{70,5},{71,8},{72,7},{7... | collective-permute-start | bytes 196616 | tf_op jit(solution)/shard_map/ppermute | solution.py:40
  182.5 10.1 %collective-permute-start.18 = (bf16[64,1024]{1,0:T(8,128)(2,1)S(1)}, bf16[64,1024]{1,0:T(8,128)(2,1)S(1)}, u32[]{:S(2)}, u32[]{:S(2)}) collective-permute-start(bf16[64,1024]{1,0:T(8,128)(2,1)S(1)} %fusion.62), channel_id=1, source_target_pairs={{64,0},{128,64},{192,128},{65,1},{129,65},{193,129},{66,2},{130,66... | collective-permute-start | bytes 393224 | tf_op jit(solution)/shard_map/ppermute | solution.py:46
  187.0 10.1 %collective-permute-start.20 = (bf16[32,1024]{1,0:T(8,128)(2,1)}, bf16[32,1024]{1,0:T(8,128)(2,1)}, u32[]{:S(2)}, u32[]{:S(2)}) collective-permute-start(bf16[32,1024]{1,0:T(8,128)(2,1)} %slice_select_fusion.7), channel_id=1, source_target_pairs={{64,63},{65,2},{66,1},{67,4},{68,3},{69,6},{70,5},{71,8},{72,7},{7... | collective-permute-start | bytes 196616 | tf_op jit(solution)/shard_map/ppermute | solution.py:40
  206.6 7.2 %collective-permute-start.21 = (bf16[64,1024]{1,0:T(8,128)(2,1)S(1)}, bf16[64,1024]{1,0:T(8,128)(2,1)S(1)}, u32[]{:S(2)}, u32[]{:S(2)}) collective-permute-start(bf16[64,1024]{1,0:T(8,128)(2,1)S(1)} %fusion.68), channel_id=1, source_target_pairs={{64,0},{128,64},{192,128},{65,1},{129,65},{193,129},{66,2},{130,66... | collective-permute-start | bytes 393224 | tf_op jit(solution)/shard_map/ppermute | solution.py:46
  208.6 9.9 %collective-permute-start.23 = (bf16[32,1024]{1,0:T(8,128)(2,1)S(1)}, bf16[32,1024]{1,0:T(8,128)(2,1)S(1)}, u32[]{:S(2)}, u32[]{:S(2)}) collective-permute-start(bf16[32,1024]{1,0:T(8,128)(2,1)S(1)} %slice_select_fusion.5), channel_id=1, source_target_pairs={{64,63},{65,2},{66,1},{67,4},{68,3},{69,6},{70,5},{71,8},{72,7},{7... | collective-permute-start | bytes 196616 | tf_op jit(solution)/shard_map/ppermute | solution.py:40
  225.1 6.9 %collective-permute-start.24 = (bf16[64,1024]{1,0:T(8,128)(2,1)S(1)}, bf16[64,1024]{1,0:T(8,128)(2,1)S(1)}, u32[]{:S(2)}, u32[]{:S(2)}) collective-permute-start(bf16[64,1024]{1,0:T(8,128)(2,1)S(1)} %fusion.74), channel_id=1, source_target_pairs={{64,0},{128,64},{192,128},{65,1},{129,65},{193,129},{66,2},{130,66... | collective-permute-start | bytes 393224 | tf_op jit(solution)/shard_map/ppermute | solution.py:46
  227.1 9.8 %collective-permute-start.26 = (bf16[32,1024]{1,0:T(8,128)(2,1)S(1)}, bf16[32,1024]{1,0:T(8,128)(2,1)S(1)}, u32[]{:S(2)}, u32[]{:S(2)}) collective-permute-start(bf16[32,1024]{1,0:T(8,128)(2,1)S(1)} %slice_select_fusion.3), channel_id=1, source_target_pairs={{64,63},{65,2},{66,1},{67,4},{68,3},{69,6},{70,5},{71,8},{72,7},{7... | collective-permute-start | bytes 196616 | tf_op jit(solution)/shard_map/ppermute | solution.py:40
  232.0 4.8 %collective-permute-start.25 = (bf16[32,1024]{1,0:T(8,128)(2,1)S(1)}, bf16[32,1024]{1,0:T(8,128)(2,1)S(1)}, u32[]{:S(2)}, u32[]{:S(2)}) collective-permute-start(bf16[32,1024]{1,0:T(8,128)(2,1)S(1)} %slice_select_fusion.4), channel_id=1, source_target_pairs={{0,1},{1,0},{2,3},{3,2},{4,5},{5,4},{6,7},{7,6},{8,9},{9,8},{10,11... | collective-permute-start | bytes 196616 | tf_op jit(solution)/shard_map/ppermute | solution.py:29
  (39 other events, 746.3 us)
Sparse Core Ops, SparseCore 0:
  11.4 84.1 all-gather.4
  194.9 24.4 all-gather.6
where the time goes:
time: 297 us; the launch traced here: 295 us
  waiting for transfers between devices  101 us (34%)
  starting transfers between devices  69.4 us (23%)
  blocking collectives  45.4 us (15%)
  matrix products  32.3 us (11%)
  other arithmetic  15.2 us (5%)
  between operations  15.2 us (5%)
  Pallas kernels  9.61 us (3%)
  local copies, waits for them, and re-layouts  7.18 us (2%)
    all_gather x1, waiting for transfers between devices, body(): lax.all_gather(master[0].astype(BF16), NODE, axis=0, tiled=True)  41.3 us
    ppermute x9, waiting for transfers between devices, beside(): return lax.ppermute(value, ('section',) + NODE, moves)  39.4 us
    ppermute x9, starting transfers between devices, beside(): return lax.ppermute(value, ('section',) + NODE, moves)  34.3 us
    all_to_all x1, blocking collectives, body(): lax.all_to_all(partial.astype(BF16).reshape(node_devs, rows, columns), NO...  29.7 us
    ppermute x8, starting transfers between devices, from_behind(): lax.ppermute(value, axis, [(source, source + steps) for source in range(l...  21.9 us
    all_to_all x1, blocking collectives, body(): lax.all_to_all(parts.transpose(1, 0, 2), PLANE, split_axis=0, concat_axis...  15.7 us
    dot_general x5, matrix products, nt(): lax.dot_general(a, b, (((1,), (1,)), ((), ())), preferred_element_type=F32)  14.6 us
    dot_general x9, matrix products, nn(): lax.dot_general(a, b, (((1,), (0,)), ((), ())), preferred_element_type=F32)  13.9 us
  transfers between devices with their start and end apart: 30, of which 16 were waited for; matrix products, arithmetic and copies ran while one was open for 9% of the time, Pallas kernels for 2%

commit v1 on v0

--- a/solution.py
+++ b/solution.py
@@ -236,16 +236,21 @@
     micro, nodes_dev, width = node_state.shape
     total_nodes = nodes_dev * node_devs
     anchor = lax.axis_index(NODE) * nodes_dev
-    weight_full = lax.all_gather(master[0].astype(BF16), NODE, axis=0, tiled=True)
+    plane = lax.axis_size(PLANE)
+    weight_rows = master.shape[1]
+    weight_full = lax.all_gather(master[0].astype(BF16), "z", axis=0, tiled=True)
+    weight_full = lax.all_gather(weight_full, PLANE, axis=0, tiled=True)
+    weight_full = weight_full.reshape(plane, node_devs // plane, weight_rows, 3 * width)
+    weight_full = weight_full.transpose(1, 0, 2, 3).reshape(width, 3 * width)
     core = lax.axis_index("core")
     side = core.astype(jnp.int32).reshape(1)
     half = nodes_dev // 2
 
-    def pair_edge(value):
-        return jnp.where(core == 0, value[..., half:, :], value[..., :half, :])
-
-    def cross_edge(value):
-        return jnp.where(core == 0, value[..., :half, :], value[..., half:, :])
+    def pair_edge(value, first):
+        return jnp.where(first, value[..., half:, :], value[..., :half, :])
+
+    def cross_edge(value, first):
+        return jnp.where(first, value[..., :half, :], value[..., half:, :])
 
     entry = route(obs_rows, obs_device, obs_node, encode_weight, node_state)
     rim = HALO_W
@@ -261,13 +266,17 @@
 
     def packed(edge):
         return jnp.concatenate(
-            [edge(head_grad).reshape(-1, width), jnp.pad(edge(near), ((0, 0), (0, width - reach)))]
+            [
+                edge(head_grad, core == 0).reshape(-1, width),
+                jnp.pad(edge(near, core == 0), ((0, 0), (0, width - reach))),
+            ]
         )
 
     from_pair = swap(packed(pair_edge))
     from_cross = beside(jnp.concatenate([packed(cross_edge), entry.reshape(-1, width)]), 0)
-    entry, from_pair, from_cross, head_grad = lax.optimization_barrier(
-        (entry, from_pair, from_cross, head_grad)
+    at_stage = [section == stage for stage in range(sections)]
+    entry, from_pair, from_cross, head_grad, first_core, side, at_stage = lax.optimization_barrier(
+        (entry, from_pair, from_cross, head_grad, core == 0, side, at_stage)
     )
     heads = micro * half
     head_pair = from_pair[:heads].reshape(micro, half, width)
@@ -275,8 +284,8 @@
     near_pair = from_pair[heads : heads + half, :reach]
     near_cross = from_cross[heads : heads + half, :reach]
     entry_cross = from_cross[heads + half :].reshape(micro, nodes_dev, width)
-    near_low = jnp.where(core == 0, near_cross, near_pair)
-    near_high = jnp.where(core == 0, near_pair, near_cross)
+    near_low = jnp.where(first_core, near_cross, near_pair)
+    near_high = jnp.where(first_core, near_pair, near_cross)
 
     def bands(upper, lower):
         room = 2 * nodes_dev - reach
@@ -296,8 +305,8 @@
         if tick == 0:
             state, cross = entry[0], entry_cross[0]
         elif tick < micro:
-            state = jnp.where(section == 0, entry[tick], incoming)
-            cross = jnp.where(section == 0, entry_cross[tick], incoming_cross)
+            state = jnp.where(at_stage[0], entry[tick], incoming)
+            cross = jnp.where(at_stage[0], entry_cross[tick], incoming_cross)
         around = jnp.concatenate([state, swap(state), cross], axis=0)
         normed = norm_rows(around.astype(F32)).astype(BF16)
         proj = nn(normed, weight_full).astype(BF16).reshape(3, nodes_dev, 3 * width)
@@ -308,16 +317,13 @@
                 kept_normed[batch] = normed[:nodes_dev]
             elif 0 < stage < sections:
                 kept_normed[batch] = jnp.where(
-                    section == stage, normed[:nodes_dev], kept_normed[batch]
+                    at_stage[stage], normed[:nodes_dev], kept_normed[batch]
                 )
         if tick + 1 < ticks:
             output = attend(side, state, proj, mask)
             incoming_cross = beside(output, 1)
             incoming = from_behind(output, "section", 1)
-    normed_all = lax.all_gather(jnp.stack(kept_normed), PLANE, axis=0, tiled=False)
-
     returning, returning_cross = None, None
-    plane = lax.axis_size(PLANE)
     columns = 3 * width // plane
     kept_grad = [None] * micro
     for tick in range(ticks):
@@ -329,31 +335,34 @@
         stages = sorted(sources)
         state, proj = saved[sources[stages[0]][1]]
         for stage in stages[1:]:
-            here = section == stage
+            here = at_stage[stage]
             state, proj = (
                 jnp.where(here, a, b) for a, b in zip(saved[sources[stage][1]], (state, proj))
             )
         last = sections - 1
         if last not in sources:
-            own, pair, cross = returning, swap(pair_edge(returning)), returning_cross
+            own, pair, cross = returning, swap(pair_edge(returning, first_core)), returning_cross
         elif tick == 0:
             own, pair, cross = head_grad[0], head_pair[0], head_cross[0]
         else:
             batch = sources[last][0]
-            own = jnp.where(section == last, head_grad[batch], returning)
-            cross = jnp.where(section == last, head_cross[batch], returning_cross)
-            pair = swap(pair_edge(own))
+            own = jnp.where(at_stage[last], head_grad[batch], returning)
+            cross = jnp.where(at_stage[last], head_cross[batch], returning_cross)
+            pair = swap(pair_edge(own, first_core))
         grad_qkv = attend_pull(side, proj, masks, own, jnp.stack([pair, cross]))
         for stage in stages:
             batch = sources[stage][0]
             if kept_grad[batch] is None:
                 kept_grad[batch] = grad_qkv
             else:
-                kept_grad[batch] = jnp.where(section == stage, grad_qkv, kept_grad[batch])
+                kept_grad[batch] = jnp.where(at_stage[stage], grad_qkv, kept_grad[batch])
         if tick + 1 < ticks:
             grad_normed = nt(grad_qkv, weight_full)
+            if tick + 2 == ticks:
+                kept, grad_normed = lax.optimization_barrier((jnp.stack(kept_normed), grad_normed))
+                normed_all = lax.all_gather(kept, PLANE, axis=0, tiled=False)
             downward = (own.astype(F32) + norm_pull(state.astype(F32), grad_normed)).astype(BF16)
-            returning_cross = beside(cross_edge(downward), -1)
+            returning_cross = beside(cross_edge(downward, first_core), -1)
             returning = from_behind(downward, "section", -1)
     parts = jnp.concatenate(kept_grad, axis=0).reshape(micro * nodes_dev, plane, columns)
     gathered = lax.all_to_all(

time: 297 us -> 287 us (0.966)
  blocking collectives: 45.4 us -> 81.2 us
  waiting for transfers between devices: 101 us -> 71.6 us
  matrix products: 32.3 us -> 23.5 us
  starting transfers between devices: 69.4 us -> 65 us
  other arithmetic: 15.2 us -> 12 us
    all_gather x2, waiting for transfers between devices: 41.3 us -> 4.91 us  [the longest x1 4.91 us: body(): weight_full = lax.all_gather(weight_full, PLANE, axis=0, tiled=True)]
    all_gather x0 -> x1, blocking collectives: none -> 31.8 us  [body(): lax.all_gather(master[0].astype(BF16), 'z', axis=0, tiled=True)]
    ppermute x10, starting transfers between devices: 1.27 us -> 8.34 us  [swap(): return lax.ppermute(value, 'core', [(0, 1), (1, 0)])]
    ppermute x8, waiting for transfers between devices: 5.56 us -> 12.2 us  [from_behind(): lax.ppermute(value, axis, [(source, source + steps) for source in range(l...]
    ppermute x9, starting transfers between devices: 34.3 us -> 28.3 us  [beside(): return lax.ppermute(value, ('section',) + NODE, moves)]
    dot_general x9, matrix products: 13.9 us -> 8.25 us  [nn(): lax.dot_general(a, b, (((1,), (0,)), ((), ())), preferred_element_type=F32)]
    all_to_all x1, blocking collectives: 29.7 us -> 33.5 us  [body(): lax.all_to_all(partial.astype(BF16).reshape(node_devs, rows, columns), NO...]
    all_to_all x1, starting transfers between devices: 11.9 us -> 8.23 us  [route(): lax.all_to_all(sent.reshape(node_devs, micro * capacity, levels + 1), NOD...]
  transfers between devices with their start and end apart: 30 -> 30, of which waited for: 16 -> 18; matrix products, arithmetic and copies ran while one was open for 9% -> 5% of each run, Pallas kernels for 2% -> 1%
where the time goes in v1:
time: 287 us; the launch traced here: 286 us
  blocking collectives  81.2 us (28%)
  waiting for transfers between devices  71.6 us (25%)
  starting transfers between devices  65 us (23%)
  matrix products  23.5 us (8%)
  between operations  15.1 us (5%)
  other arithmetic  12 us (4%)
  Pallas kernels  9.61 us (3%)
  local copies, waits for them, and re-layouts  7.95 us (3%)
    ppermute x9, waiting for transfers between devices, beside(): return lax.ppermute(value, ('section',) + NODE, moves)  40.2 us
    all_to_all x1, blocking collectives, body(): lax.all_to_all(partial.astype(BF16).reshape(node_devs, rows, columns), NO...  33.5 us
    all_gather x1, blocking collectives, body(): lax.all_gather(master[0].astype(BF16), 'z', axis=0, tiled=True)  31.8 us
    ppermute x9, starting transfers between devices, beside(): return lax.ppermute(value, ('section',) + NODE, moves)  28.3 us
    ppermute x8, starting transfers between devices, from_behind(): lax.ppermute(value, axis, [(source, source + steps) for source in range(l...  20 us
    all_to_all x1, blocking collectives, body(): lax.all_to_all(parts.transpose(1, 0, 2), PLANE, split_axis=0, concat_axis...  16 us
    dot_general x5, matrix products, nt(): lax.dot_general(a, b, (((1,), (1,)), ((), ())), preferred_element_type=F32)  12.2 us
    ppermute x8, waiting for transfers between devices, from_behind(): lax.ppermute(value, axis, [(source, source + steps) for source in range(l...  12.2 us
  transfers between devices with their start and end apart: 30, of which 18 were waited for; matrix products, arithmetic and copies ran while one was open for 5% of the time, Pallas kernels for 1%

profile of v1, /device:TPU:8, one launch (start us, length us, event | category | flops | bytes accessed | tf_op | source)
XLA Modules:
  0.0 285.9 jit_solution(16275186401629399334)
XLA Ops:
  8.3 31.8 %all-gather = bf16[1,128,3072]{2,1,0:T(8,128)(2,1)} all-gather(bf16[1,16,3072]{2,1,0:T(8,128)(2,1)S(1)} %convert_element_type.200), channel_id=2, replica_groups=mesh['section'=4,'z'=8,'x'=4,'core'=2] {'z'}, dimensions={1}, use_global_device_ids=true | all-gather | bytes 884736 | tf_op jit(solution)/shard_map/all_gather | solution.py:241
  43.2 8.2 %all-to-all-start = ((bf16[64,8,248]{2,1,0:T(8,128)(2,1)}), bf16[64,8,248]{2,1,0:T(8,128)(2,1)S(1)}, u32[]{:S(2)}, u32[]{:S(2)}) async-start(bf16[64,8,248]{2,1,0:T(8,128)(2,1)} %bitcast.6), calls=%async_computation | async-start | bytes 524288 | tf_op jit(solution)/shard_map/all_to_all | solution.py:202
  52.4 12.0 %all-to-all-done = bf16[64,8,248]{2,1,0:T(8,128)(2,1)S(1)} async-done(((bf16[64,8,248]{2,1,0:T(8,128)(2,1)}), bf16[64,8,248]{2,1,0:T(8,128)(2,1)S(1)}, u32[]{:S(2)}, u32[]{:S(2)}) %all-to-all-start) | async-done | bytes 253984 | tf_op jit(solution)/shard_map/all_to_all | solution.py:202
  68.6 8.4 %collective-permute-done.1 = bf16[224,1024]{1,0:T(8,128)(2,1)S(1)} collective-permute-done((bf16[224,1024]{1,0:T(8,128)(2,1)S(1)}, bf16[224,1024]{1,0:T(8,128)(2,1)S(1)}, u32[]{:S(2)}, u32[]{:S(2)}) %collective-permute-start.1) | collective-permute-done | bytes 458784 | tf_op jit(solution)/shard_map/ppermute | solution.py:40
  77.0 7.1 %collective-permute-start.2 = (bf16[64,1024]{1,0:T(8,128)(2,1)S(1)}, bf16[64,1024]{1,0:T(8,128)(2,1)S(1)}, u32[]{:S(2)}, u32[]{:S(2)}) collective-permute-start(bf16[64,1024]{1,0:T(8,128)(2,1)S(1)} %slice_bitcast_fusion.1.state_ref), channel_id=1, source_target_pairs={{0,1},{1,0},{2,3},{3,2},{4,5},{5,4},{6,7},{7,6},{8,9},{9,8},{10,11... | collective-permute-start | bytes 393224 | tf_op jit(solution)/shard_map/ppermute | solution.py:29
  85.4 4.9 %all-gather.6.cloned.1.call-done = bf16[1,1024,3072]{2,1,0:T(8,128)(2,1)} async-done(((bf16[1,128,3072]{2,1,0:T(8,128)(2,1)}), bf16[1,1024,3072]{2,1,0:T(8,128)(2,1)}) %all-gather.6.cloned.1.call-update) | async-done | bytes 6291472 | tf_op jit(solution)/shard_map/all_gather | solution.py:242
  90.4 3.2 %copy.34 = bf16[8,8,16,3072]{3,2,1,0:T(8,128)(2,1)S(1)} copy(bf16[8,8,16,3072]{3,2,0,1:T(8,128)(2,1)} %bitcast.143) | data formatting | bytes 12582912 | tf_op jit(solution)/shard_map/transpose | solution.py:244
  95.6 3.4 %collective-permute-start.3 = (bf16[64,1024]{1,0:T(8,128)(2,1)S(1)}, bf16[64,1024]{1,0:T(8,128)(2,1)S(1)}, u32[]{:S(2)}, u32[]{:S(2)}) collective-permute-start(bf16[64,1024]{1,0:T(8,128)(2,1)S(1)} %attend.4), channel_id=1, source_target_pairs={{0,64},{64,128},{128,192},{1,65},{65,129},{129,193},{2,66},{66,130... | collective-permute-start | bytes 393224 | tf_op jit(solution)/shard_map/ppermute | solution.py:46
  99.1 5.5 %collective-permute-start.5 = (bf16[64,1024]{1,0:T(8,128)(2,1)S(1)}, bf16[64,1024]{1,0:T(8,128)(2,1)S(1)}, u32[]{:S(2)}, u32[]{:S(2)}) collective-permute-start(bf16[64,1024]{1,0:T(8,128)(2,1)S(1)} %attend.4), channel_id=1, source_target_pairs={{0,127},{1,66},{2,65},{3,68},{4,67},{5,70},{6,69},{7,72},{8,71},{9... | collective-permute-start | bytes 393224 | tf_op jit(solution)/shard_map/ppermute | solution.py:40
  104.7 4.8 %collective-permute-done.5 = bf16[64,1024]{1,0:T(8,128)(2,1)S(1)} collective-permute-done((bf16[64,1024]{1,0:T(8,128)(2,1)S(1)}, bf16[64,1024]{1,0:T(8,128)(2,1)S(1)}, u32[]{:S(2)}, u32[]{:S(2)}) %collective-permute-start.5) | collective-permute-done | bytes 131104 | tf_op jit(solution)/shard_map/ppermute | solution.py:40
  111.9 3.1 %collective-permute-start.6 = (bf16[64,1024]{1,0:T(8,128)(2,1)S(1)}, bf16[64,1024]{1,0:T(8,128)(2,1)S(1)}, u32[]{:S(2)}, u32[]{:S(2)}) collective-permute-start(bf16[64,1024]{1,0:T(8,128)(2,1)S(1)} %attend.5), channel_id=1, source_target_pairs={{0,64},{64,128},{128,192},{1,65},{65,129},{129,193},{2,66},{66,130... | collective-permute-start | bytes 393224 | tf_op jit(solution)/shard_map/ppermute | solution.py:46
  115.0 4.3 %collective-permute-start.8 = (bf16[64,1024]{1,0:T(8,128)(2,1)S(1)}, bf16[64,1024]{1,0:T(8,128)(2,1)S(1)}, u32[]{:S(2)}, u32[]{:S(2)}) collective-permute-start(bf16[64,1024]{1,0:T(8,128)(2,1)S(1)} %attend.5), channel_id=1, source_target_pairs={{0,127},{1,66},{2,65},{3,68},{4,67},{5,70},{6,69},{7,72},{8,71},{9... | collective-permute-start | bytes 393224 | tf_op jit(solution)/shard_map/ppermute | solution.py:40
  120.2 5.3 %collective-permute-done.8 = bf16[64,1024]{1,0:T(8,128)(2,1)S(1)} collective-permute-done((bf16[64,1024]{1,0:T(8,128)(2,1)S(1)}, bf16[64,1024]{1,0:T(8,128)(2,1)S(1)}, u32[]{:S(2)}, u32[]{:S(2)}) %collective-permute-start.8) | collective-permute-done | bytes 131104 | tf_op jit(solution)/shard_map/ppermute | solution.py:40
  129.8 4.3 %collective-permute-start.11 = (bf16[64,1024]{1,0:T(8,128)(2,1)S(1)}, bf16[64,1024]{1,0:T(8,128)(2,1)S(1)}, u32[]{:S(2)}, u32[]{:S(2)}) collective-permute-start(bf16[64,1024]{1,0:T(8,128)(2,1)S(1)} %attend.6), channel_id=1, source_target_pairs={{0,127},{1,66},{2,65},{3,68},{4,67},{5,70},{6,69},{7,72},{8,71},{9... | collective-permute-start | bytes 393224 | tf_op jit(solution)/shard_map/ppermute | solution.py:40
  135.5 4.8 %collective-permute-done.11 = bf16[64,1024]{1,0:T(8,128)(2,1)S(1)} collective-permute-done((bf16[64,1024]{1,0:T(8,128)(2,1)S(1)}, bf16[64,1024]{1,0:T(8,128)(2,1)S(1)}, u32[]{:S(2)}, u32[]{:S(2)}) %collective-permute-start.11) | collective-permute-done | bytes 131104 | tf_op jit(solution)/shard_map/ppermute | solution.py:40
  142.6 4.3 %collective-permute-start.14 = (bf16[64,1024]{1,0:T(8,128)(2,1)S(1)}, bf16[64,1024]{1,0:T(8,128)(2,1)S(1)}, u32[]{:S(2)}, u32[]{:S(2)}) collective-permute-start(bf16[64,1024]{1,0:T(8,128)(2,1)S(1)} %attend.7), channel_id=1, source_target_pairs={{0,127},{1,66},{2,65},{3,68},{4,67},{5,70},{6,69},{7,72},{8,71},{9... | collective-permute-start | bytes 393224 | tf_op jit(solution)/shard_map/ppermute | solution.py:40
  152.8 3.9 %collective-permute-start.15 = (bf16[64,1024]{1,0:T(8,128)(2,1)S(1)}, bf16[64,1024]{1,0:T(8,128)(2,1)S(1)}, u32[]{:S(2)}, u32[]{:S(2)}) collective-permute-start(bf16[64,1024]{1,0:T(8,128)(2,1)S(1)} %fusion.23), channel_id=1, source_target_pairs={{64,0},{128,64},{192,128},{65,1},{129,65},{193,129},{66,2},{130,66... | collective-permute-start | bytes 393224 | tf_op jit(solution)/shard_map/ppermute | solution.py:46
  160.3 6.3 %collective-permute-done.17 = bf16[32,1024]{1,0:T(8,128)(2,1)S(1)} collective-permute-done((bf16[32,1024]{1,0:T(8,128)(2,1)S(1)}, bf16[32,1024]{1,0:T(8,128)(2,1)S(1)}, u32[]{:S(2)}, u32[]{:S(2)}) %collective-permute-start.17) | collective-permute-done | bytes 65568 | tf_op jit(solution)/shard_map/ppermute | solution.py:40
  180.5 3.8 %collective-permute-done.20 = bf16[32,1024]{1,0:T(8,128)(2,1)S(1)} collective-permute-done((bf16[32,1024]{1,0:T(8,128)(2,1)S(1)}, bf16[32,1024]{1,0:T(8,128)(2,1)S(1)}, u32[]{:S(2)}, u32[]{:S(2)}) %collective-permute-start.20) | collective-permute-done | bytes 65568 | tf_op jit(solution)/shard_map/ppermute | solution.py:40
  204.1 5.5 %fusion.80 = f32[64,1024]{1,0:T(8,128)} fusion(bf16[64,3072]{1,0:T(8,128)(2,1)S(1)} %attend_pull.8, bf16[1024,3072]{1,0:T(8,128)(2,1)} %bitcast.142), kind=kOutput, calls=%fused_computation.212 | convolution fusion | flops 402653184 | bytes 6946816 | tf_op jit(solution)/shard_map/dot_general | solution.py:60
  215.9 3.7 %collective-permute-done.24.own_ref = bf16[64,1024]{1,0:T(8,128)(2,1)S(1)} collective-permute-done((bf16[64,1024]{1,0:T(8,128)(2,1)S(1)}, bf16[64,1024]{1,0:T(8,128)(2,1)S(1)}, u32[]{:S(2)}, u32[]{:S(2)}) %collective-permute-start.24) | collective-permute-done | bytes 131104 | tf_op jit(solution)/shard_map/ppermute | solution.py:46
  219.9 3.8 %collective-permute-done.26 = bf16[32,1024]{1,0:T(8,128)(2,1)S(1)} collective-permute-done((bf16[32,1024]{1,0:T(8,128)(2,1)S(1)}, bf16[32,1024]{1,0:T(8,128)(2,1)S(1)}, u32[]{:S(2)}, u32[]{:S(2)}) %collective-permute-start.26) | collective-permute-done | bytes 65568 | tf_op jit(solution)/shard_map/ppermute | solution.py:40
  225.6 16.0 %all_to_all.15 = bf16[8,128,384]{2,1,0:T(8,128)(2,1)S(1)} all-to-all(bf16[8,128,384]{2,1,0:T(8,128)(2,1)S(1)} %bitcast.150), channel_id=1, replica_groups=mesh['section'=4,'z'=8,'x'=4,'core'=2] {'x','core'}, dimensions={0} | all-to-all | bytes 1572864 | tf_op jit(solution)/shard_map/all_to_all | solution.py:368
  244.5 33.5 %all_to_all.16 = bf16[64,16,384]{2,1,0:T(8,128)(2,1)S(1)} all-to-all(bf16[64,16,384]{2,1,0:T(8,128)(2,1)S(1)} %bitcast.155), channel_id=1, replica_groups=mesh['section'=4,'z'=8,'x'=4,'core'=2] {'z','x','core'}, dimensions={0} | all-to-all | bytes 1572864 | tf_op jit(solution)/shard_map/all_to_all | solution.py:376
  (190 shorter events, 78.7 us)
Async XLA Ops:
  7.2 83.1 %all-gather.6.cloned.1.call-start = ((), (), s32[]{:S(2)}) async-start(), calls=%async_computation.3 | async-start | bytes 7077888 | tf_op jit(solution)/shard_map/all_gather | solution.py:242
  43.2 21.2 %all-to-all-start = ((bf16[64,8,248]{2,1,0:T(8,128)(2,1)}), bf16[64,8,248]{2,1,0:T(8,128)(2,1)S(1)}, u32[]{:S(2)}, u32[]{:S(2)}) async-start(bf16[64,8,248]{2,1,0:T(8,128)(2,1)} %bitcast.6), calls=%async_computation | async-start | bytes 524288 | tf_op jit(solution)/shard_map/all_to_all | solution.py:202
  51.4 190.1 %all-gather.8.cloned.1.call-start = ((), (), s32[]{:S(2)}) async-start(), calls=%async_computation.4 | async-start | bytes 2359296 | tf_op jit(solution)/shard_map/all_gather | solution.py:363
  65.6 11.4 %collective-permute-start.1 = (bf16[224,1024]{1,0:T(8,128)(2,1)S(1)}, bf16[224,1024]{1,0:T(8,128)(2,1)S(1)}, u32[]{:S(2)}, u32[]{:S(2)}) collective-permute-start(bf16[224,1024]{1,0:T(8,128)(2,1)S(1)} %fusion.16), channel_id=1, source_target_pairs={{0,63},{1,2},{2,1},{3,4},{4,3},{5,6},{6,5},{7,8},{8,7},{9,10},{10,... | collective-permute-start | bytes 1376264 | tf_op jit(solution)/shard_map/ppermute | solution.py:40
  77.0 8.1 %collective-permute-start.2 = (bf16[64,1024]{1,0:T(8,128)(2,1)S(1)}, bf16[64,1024]{1,0:T(8,128)(2,1)S(1)}, u32[]{:S(2)}, u32[]{:S(2)}) collective-permute-start(bf16[64,1024]{1,0:T(8,128)(2,1)S(1)} %slice_bitcast_fusion.1.state_ref), channel_id=1, source_target_pairs={{0,1},{1,0},{2,3},{3,2},{4,5},{5,4},{6,7},{7,6},{8,9},{9,8},{10,11... | collective-permute-start | bytes 393224 | tf_op jit(solution)/shard_map/ppermute | solution.py:29
  95.6 9.0 %collective-permute-start.3 = (bf16[64,1024]{1,0:T(8,128)(2,1)S(1)}, bf16[64,1024]{1,0:T(8,128)(2,1)S(1)}, u32[]{:S(2)}, u32[]{:S(2)}) collective-permute-start(bf16[64,1024]{1,0:T(8,128)(2,1)S(1)} %attend.4), channel_id=1, source_target_pairs={{0,64},{64,128},{128,192},{1,65},{65,129},{129,193},{2,66},{66,130... | collective-permute-start | bytes 393224 | tf_op jit(solution)/shard_map/ppermute | solution.py:46
  99.1 10.5 %collective-permute-start.5 = (bf16[64,1024]{1,0:T(8,128)(2,1)S(1)}, bf16[64,1024]{1,0:T(8,128)(2,1)S(1)}, u32[]{:S(2)}, u32[]{:S(2)}) collective-permute-start(bf16[64,1024]{1,0:T(8,128)(2,1)S(1)} %attend.4), channel_id=1, source_target_pairs={{0,127},{1,66},{2,65},{3,68},{4,67},{5,70},{6,69},{7,72},{8,71},{9... | collective-permute-start | bytes 393224 | tf_op jit(solution)/shard_map/ppermute | solution.py:40
  111.9 8.3 %collective-permute-start.6 = (bf16[64,1024]{1,0:T(8,128)(2,1)S(1)}, bf16[64,1024]{1,0:T(8,128)(2,1)S(1)}, u32[]{:S(2)}, u32[]{:S(2)}) collective-permute-start(bf16[64,1024]{1,0:T(8,128)(2,1)S(1)} %attend.5), channel_id=1, source_target_pairs={{0,64},{64,128},{128,192},{1,65},{65,129},{129,193},{2,66},{66,130... | collective-permute-start | bytes 393224 | tf_op jit(solution)/shard_map/ppermute | solution.py:46
  115.0 10.5 %collective-permute-start.8 = (bf16[64,1024]{1,0:T(8,128)(2,1)S(1)}, bf16[64,1024]{1,0:T(8,128)(2,1)S(1)}, u32[]{:S(2)}, u32[]{:S(2)}) collective-permute-start(bf16[64,1024]{1,0:T(8,128)(2,1)S(1)} %attend.5), channel_id=1, source_target_pairs={{0,127},{1,66},{2,65},{3,68},{4,67},{5,70},{6,69},{7,72},{8,71},{9... | collective-permute-start | bytes 393224 | tf_op jit(solution)/shard_map/ppermute | solution.py:40
  120.1 5.4 %collective-permute-start.7 = (bf16[64,1024]{1,0:T(8,128)(2,1)S(1)}, bf16[64,1024]{1,0:T(8,128)(2,1)S(1)}, u32[]{:S(2)}, u32[]{:S(2)}) collective-permute-start(bf16[64,1024]{1,0:T(8,128)(2,1)S(1)} %collective-permute-done.6.state_ref), channel_id=1, source_target_pairs={{0,1},{1,0},{2,3},{3,2},{4,5},{5,4},{6,7},{7,6},{8,9},{9,8},{10,11... | collective-permute-start | bytes 393224 | tf_op jit(solution)/shard_map/ppermute | solution.py:29
  127.8 7.7 %collective-permute-start.9 = (bf16[64,1024]{1,0:T(8,128)(2,1)S(1)}, bf16[64,1024]{1,0:T(8,128)(2,1)S(1)}, u32[]{:S(2)}, u32[]{:S(2)}) collective-permute-start(bf16[64,1024]{1,0:T(8,128)(2,1)S(1)} %attend.6), channel_id=1, source_target_pairs={{0,64},{64,128},{128,192},{1,65},{65,129},{129,193},{2,66},{66,130... | collective-permute-start | bytes 393224 | tf_op jit(solution)/shard_map/ppermute | solution.py:46
  129.8 10.5 %collective-permute-start.11 = (bf16[64,1024]{1,0:T(8,128)(2,1)S(1)}, bf16[64,1024]{1,0:T(8,128)(2,1)S(1)}, u32[]{:S(2)}, u32[]{:S(2)}) collective-permute-start(bf16[64,1024]{1,0:T(8,128)(2,1)S(1)} %attend.6), channel_id=1, source_target_pairs={{0,127},{1,66},{2,65},{3,68},{4,67},{5,70},{6,69},{7,72},{8,71},{9... | collective-permute-start | bytes 393224 | tf_op jit(solution)/shard_map/ppermute | solution.py:40
  142.6 24.1 %collective-permute-start.14 = (bf16[64,1024]{1,0:T(8,128)(2,1)S(1)}, bf16[64,1024]{1,0:T(8,128)(2,1)S(1)}, u32[]{:S(2)}, u32[]{:S(2)}) collective-permute-start(bf16[64,1024]{1,0:T(8,128)(2,1)S(1)} %attend.7), channel_id=1, source_target_pairs={{0,127},{1,66},{2,65},{3,68},{4,67},{5,70},{6,69},{7,72},{8,71},{9... | collective-permute-start | bytes 393224 | tf_op jit(solution)/shard_map/ppermute | solution.py:40
  147.0 12.9 %collective-permute-start.12 = (bf16[64,1024]{1,0:T(8,128)(2,1)S(1)}, bf16[64,1024]{1,0:T(8,128)(2,1)S(1)}, u32[]{:S(2)}, u32[]{:S(2)}) collective-permute-start(bf16[64,1024]{1,0:T(8,128)(2,1)S(1)} %attend.7), channel_id=1, source_target_pairs={{0,64},{64,128},{128,192},{1,65},{65,129},{129,193},{2,66},{66,130... | collective-permute-start | bytes 393224 | tf_op jit(solution)/shard_map/ppermute | solution.py:46
  152.8 6.9 %collective-permute-start.15 = (bf16[64,1024]{1,0:T(8,128)(2,1)S(1)}, bf16[64,1024]{1,0:T(8,128)(2,1)S(1)}, u32[]{:S(2)}, u32[]{:S(2)}) collective-permute-start(bf16[64,1024]{1,0:T(8,128)(2,1)S(1)} %fusion.23), channel_id=1, source_target_pairs={{64,0},{128,64},{192,128},{65,1},{129,65},{193,129},{66,2},{130,66... | collective-permute-start | bytes 393224 | tf_op jit(solution)/shard_map/ppermute | solution.py:46
  156.8 9.8 %collective-permute-start.17 = (bf16[32,1024]{1,0:T(8,128)(2,1)S(1)}, bf16[32,1024]{1,0:T(8,128)(2,1)S(1)}, u32[]{:S(2)}, u32[]{:S(2)}) collective-permute-start(bf16[32,1024]{1,0:T(8,128)(2,1)S(1)} %slice_select_fusion.9), channel_id=1, source_target_pairs={{64,63},{65,2},{66,1},{67,4},{68,3},{69,6},{70,5},{71,8},{72,7},{7... | collective-permute-start | bytes 196616 | tf_op jit(solution)/shard_map/ppermute | solution.py:40
  159.7 6.9 %collective-permute-start.16 = (bf16[32,1024]{1,0:T(8,128)(2,1)S(1)}, bf16[32,1024]{1,0:T(8,128)(2,1)S(1)}, u32[]{:S(2)}, u32[]{:S(2)}) collective-permute-start(bf16[32,1024]{1,0:T(8,128)(2,1)S(1)} %slice_select_fusion.10), channel_id=1, source_target_pairs={{0,1},{1,0},{2,3},{3,2},{4,5},{5,4},{6,7},{7,6},{8,9},{9,8},{10,11... | collective-permute-start | bytes 196616 | tf_op jit(solution)/shard_map/ppermute | solution.py:29
  159.9 6.8 %collective-permute-start.13 = (bf16[64,1024]{1,0:T(8,128)(2,1)S(1)}, bf16[64,1024]{1,0:T(8,128)(2,1)S(1)}, u32[]{:S(2)}, u32[]{:S(2)}) collective-permute-start(bf16[64,1024]{1,0:T(8,128)(2,1)S(1)} %collective-permute-done.12), channel_id=1, source_target_pairs={{0,1},{1,0},{2,3},{3,2},{4,5},{5,4},{6,7},{7,6},{8,9},{9,8},{10,11... | collective-permute-start | bytes 393224 | tf_op jit(solution)/shard_map/ppermute | solution.py:29
  172.5 6.9 %collective-permute-start.18 = (bf16[64,1024]{1,0:T(8,128)(2,1)S(1)}, bf16[64,1024]{1,0:T(8,128)(2,1)S(1)}, u32[]{:S(2)}, u32[]{:S(2)}) collective-permute-start(bf16[64,1024]{1,0:T(8,128)(2,1)S(1)} %fusion.29), channel_id=1, source_target_pairs={{64,0},{128,64},{192,128},{65,1},{129,65},{193,129},{66,2},{130,66... | collective-permute-start | bytes 393224 | tf_op jit(solution)/shard_map/ppermute | solution.py:46
  174.5 9.8 %collective-permute-start.20 = (bf16[32,1024]{1,0:T(8,128)(2,1)S(1)}, bf16[32,1024]{1,0:T(8,128)(2,1)S(1)}, u32[]{:S(2)}, u32[]{:S(2)}) collective-permute-start(bf16[32,1024]{1,0:T(8,128)(2,1)S(1)} %slice_select_fusion.7), channel_id=1, source_target_pairs={{64,63},{65,2},{66,1},{67,4},{68,3},{69,6},{70,5},{71,8},{72,7},{7... | collective-permute-start | bytes 196616 | tf_op jit(solution)/shard_map/ppermute | solution.py:40
  188.1 6.9 %collective-permute-start.21 = (bf16[64,1024]{1,0:T(8,128)(2,1)S(1)}, bf16[64,1024]{1,0:T(8,128)(2,1)S(1)}, u32[]{:S(2)}, u32[]{:S(2)}) collective-permute-start(bf16[64,1024]{1,0:T(8,128)(2,1)S(1)} %fusion.35), channel_id=1, source_target_pairs={{64,0},{128,64},{192,128},{65,1},{129,65},{193,129},{66,2},{130,66... | collective-permute-start | bytes 393224 | tf_op jit(solution)/shard_map/ppermute | solution.py:46
  190.1 9.9 %collective-permute-start.23 = (bf16[32,1024]{1,0:T(8,128)(2,1)S(1)}, bf16[32,1024]{1,0:T(8,128)(2,1)}, u32[]{:S(2)}, u32[]{:S(2)}) collective-permute-start(bf16[32,1024]{1,0:T(8,128)(2,1)S(1)} %slice_select_fusion.5), channel_id=1, source_target_pairs={{64,63},{65,2},{66,1},{67,4},{68,3},{69,6},{70,5},{71,8},{72,7},{7... | collective-permute-start | bytes 196616 | tf_op jit(solution)/shard_map/ppermute | solution.py:40
  212.0 7.6 %collective-permute-start.24 = (bf16[64,1024]{1,0:T(8,128)(2,1)S(1)}, bf16[64,1024]{1,0:T(8,128)(2,1)S(1)}, u32[]{:S(2)}, u32[]{:S(2)}) collective-permute-start(bf16[64,1024]{1,0:T(8,128)(2,1)S(1)} %fusion.41), channel_id=1, source_target_pairs={{64,0},{128,64},{192,128},{65,1},{129,65},{193,129},{66,2},{130,66... | collective-permute-start | bytes 393224 | tf_op jit(solution)/shard_map/ppermute | solution.py:46
  213.9 9.8 %collective-permute-start.26 = (bf16[32,1024]{1,0:T(8,128)(2,1)S(1)}, bf16[32,1024]{1,0:T(8,128)(2,1)S(1)}, u32[]{:S(2)}, u32[]{:S(2)}) collective-permute-start(bf16[32,1024]{1,0:T(8,128)(2,1)S(1)} %slice_select_fusion.3), channel_id=1, source_target_pairs={{64,63},{65,2},{66,1},{67,4},{68,3},{69,6},{70,5},{71,8},{72,7},{7... | collective-permute-start | bytes 196616 | tf_op jit(solution)/shard_map/ppermute | solution.py:40
  (27 other events, 602.7 us)
Sparse Core Ops, SparseCore 0:
  40.2 50.0 all-gather.5
  209.7 28.0 all-gather.7
